TPU v7x, 32 devices: a whole 2x2x4 slice. The times are simulated.
32 devices in a mesh: worker: 4 (over z), fsdp: 8 (over y, x, core).
Axes of the slice: x: 2, y: 2, z: 4, core: 2. Of those that a mesh axis runs over, the one named last changes fastest.
Arguments:
- outer_weights: float32 [4, 2, 2048, 512], P('worker', None, 'fsdp'), may hold values from -6 to 6
- pseudo_grad: float32 [4, 2, 2048, 512], P('worker', None, 'fsdp'), may hold values from -6 to 6
- momentum: float32 [4, 2, 2048, 512], P('worker', None, 'fsdp'), may hold values from -6 to 6
- partner: int32 [4], replicated, may hold values from 0 to 3, as said below
Outputs:
- momentum_next: float32 [4, 2, 2048, 512], P('worker', None, 'fsdp')
- weights_full: bfloat16 [4, 2, 2048, 512], P('worker')
Inputs may be any that keep to these rules, and one draw needn't show every extreme that they name: partner[partner[w]] = w and partner[w] != w for every replica w.
All inputs are finite; a program needn't handle non-finite values.
Results may differ from a plain program's by a relative error of at most 0.001.
Values may be sent and summed in bfloat16 or wider, within the bound.
A program may use at most 64 MiB of HBM per device.

v0:
```python
import functools

import jax
import jax.numpy as jnp
from jax import lax
from jax.experimental import pallas as pl
from jax.experimental.pallas import tpu as pltpu
from jax.sharding import PartitionSpec as P

MESH = pl.DeviceIdType.MESH

momentum_decay = 0.9
outer_rate = 0.7
pull_rate = 0.6

LANES = 128
SUB = 8
STEPS = 32767.0
PARTS = 8
LAG = 2
SLICES = 4


def finish(weights, moment, pair_delta, pair_weights):
    moment_next = momentum_decay * moment + pair_delta
    new_weights = (
        weights
        - outer_rate * (momentum_decay * moment_next + pair_delta)
        - pull_rate * (weights - pair_weights)
    )
    return (new_weights, moment_next)


def gathered_body(outer_weights, pseudo_grad, momentum, partner):
    mate_index = partner[lax.axis_index("worker")]
    pieces = (
        lax.all_gather(outer_weights, "worker", axis=0, tiled=True),
        lax.all_gather(pseudo_grad, "worker", axis=0, tiled=True),
    )
    first = lax.dynamic_slice_in_dim(pieces[0], mate_index, 1, 0)
    second = lax.dynamic_slice_in_dim(pieces[1], mate_index, 1, 0)
    pair_delta = (pseudo_grad + second) * 0.5
    pair_weights = (outer_weights + first) * 0.5
    new_weights, moment_next = finish(outer_weights, momentum, pair_delta, pair_weights)
    weights_full = lax.all_gather(new_weights.astype(jnp.bfloat16), "fsdp", axis=2, tiled=True)
    return (moment_next, weights_full)


def mate_of(worker, matching):
    if matching == 1:
        return worker + 1 - 2 * lax.rem(worker, 2)
    if matching == 2:
        return lax.rem(worker + 2, 4)
    return 3 - worker


def pair_kernel(
    matching, mats,
    w_hbm, g_hbm, m_hbm,
    next_ref, full_ref,
    w_ref, g_ref, m_ref, scale_out, scale_in, q_out, q_in,
    load_sem, scale_send, scale_recv, q_send, q_recv,
    direct_send, direct_recv, core_send, core_recv,
):
    total, cols = w_ref.shape
    rows = total // mats
    height = total // PARTS
    per_mat = rows // height
    groups = height // SUB
    pieces = cols // LANES
    all_rows = full_ref.shape[0] // mats

    worker, spot = lax.axis_index("worker"), lax.axis_index("fsdp")
    mate = mate_of(worker, matching)
    core = lax.rem(spot, 2)
    chip = lax.div(spot, 2)
    along_x, along_y = lax.rem(chip, 2), lax.div(chip, 2)

    def place(x, y, c):
        return (y * 2 + x) * 2 + c

    chips = (
        (along_x, along_y),
        (1 - along_x, along_y),
        (along_x, 1 - along_y),
        (1 - along_x, 1 - along_y),
    )
    twins = [place(x, y, core) for x, y in chips]
    neighbour = place(along_x, along_y, 1 - core)
    peers = [(mate, spot), (worker, neighbour)] + [(worker, t) for t in twins[1:]]

    def load(source, target, first, count, number):
        return pltpu.make_async_copy(
            source.at[pl.ds(first, count)], target.at[pl.ds(first, count)], load_sem.at[number]
        )

    loads = [
        load(w_hbm, w_ref, 0, height, 0),
        load(g_hbm, g_ref, 0, height, 1),
        load(w_hbm, w_ref, height, total - height, 2),
        load(g_hbm, g_ref, height, total - height, 3),
        load(m_hbm, m_ref, 0, total, 4),
    ]
    for copy in loads:
        copy.start()

    barrier = pltpu.get_barrier_semaphore()
    for peer in peers:
        pl.semaphore_signal(barrier, inc=1, device_id=peer, device_id_type=MESH)

    def at(part):
        return pl.ds(pl.multiple_of(part * height, height), height)

    def to_mate(part):
        return [
            pltpu.make_async_remote_copy(
                out.at[part], into.at[part], sent.at[part], came.at[part],
                device_id=(mate, spot), device_id_type=MESH,
            )
            for out, into, sent, came in (
                (scale_out, scale_in, scale_send, scale_recv),
                (q_out, q_in, q_send, q_recv),
            )
        ]

    def code(part):
        for number, ref in enumerate((w_ref, g_ref)):
            tiles = [
                ref[at(part), piece * LANES : (piece + 1) * LANES].reshape(groups, SUB, LANES)
                for piece in range(pieces)
            ]
            top = jnp.full((SUB, LANES), 1e-30, jnp.float32)
            for tile in tiles:
                top = jnp.maximum(top, jnp.max(jnp.abs(tile), axis=0))
            scale_out[part, number] = top
            inverse = STEPS / top
            for piece, tile in enumerate(tiles):
                level = (tile * inverse[None] + 32768.5).astype(jnp.int32) - 32768
                q_out[part, number, :, piece * LANES : (piece + 1) * LANES] = level.reshape(height, LANES).astype(
                    jnp.int16
                )

    def send(part):
        for copy in to_mate(part):
            copy.start()

    loads[0].wait()
    loads[1].wait()
    code(0)
    pl.semaphore_wait(barrier, len(peers))
    send(0)
    loads[2].wait()
    loads[3].wait()

    def code_and_send(part, _):
        code(part)
        send(part)
        return 0

    lax.fori_loop(1, PARTS, code_and_send, 0)
    loads[4].wait()

    def first_row(owner, part):
        mat, first = lax.div(part, per_mat), lax.rem(part, per_mat) * height
        return pl.multiple_of(mat * all_rows + owner * rows + first, height)

    def rows_of(owner, part):
        return full_ref.at[pl.ds(first_row(owner, part), height)]

    def direct(part, way):
        return pltpu.make_async_remote_copy(
            rows_of(spot, part), rows_of(spot, part), direct_send.at[way - 1, part], direct_recv.at[way - 1, part],
            device_id=(worker, twins[way]), device_id_type=MESH,
        )

    def across_cores(part, way):
        return pltpu.make_async_remote_copy(
            rows_of(twins[way], part), rows_of(twins[way], part), core_send.at[way, part], core_recv.at[way, part],
            device_id=(worker, neighbour), device_id_type=MESH,
        )

    def update(part):
        for copy in to_mate(part):
            copy.wait_recv()
        back = [scale_in[part, number] * (1.0 / STEPS) for number in range(2)]
        mine = pl.ds(first_row(spot, part), height)
        for piece in range(pieces):
            lanes = slice(piece * LANES, (piece + 1) * LANES)
            got = [
                (
                    q_in[part, number, :, lanes].astype(jnp.int32).astype(jnp.float32).reshape(groups, SUB, LANES)
                    * back[number][None]
                ).reshape(height, LANES)
                for number in range(2)
            ]
            weights, delta, moment = (ref[at(part), lanes] for ref in (w_ref, g_ref, m_ref))
            new, moment_next = finish(weights, moment, (delta + got[1]) * 0.5, (weights + got[0]) * 0.5)
            next_ref[at(part), lanes] = moment_next
            full_ref[mine, lanes] = new.astype(jnp.bfloat16)
        for way in (3, 1, 2):
            direct(part, way).start()
        across_cores(part, 0).start()

    def pass_on(part):
        for way in (1, 2, 3):
            direct(part, way).wait_recv()
            across_cores(part, way).start()

    def head(part, _):
        update(part)
        return 0

    def both(part, _):
        update(part)
        pass_on(part - LAG)
        return 0

    def tail(part, _):
        pass_on(part)
        return 0

    lax.fori_loop(0, LAG, head, 0)
    lax.fori_loop(LAG, PARTS, both, 0)
    lax.fori_loop(PARTS - LAG, PARTS, tail, 0)

    def drain(part, _):
        for copy in to_mate(part):
            copy.wait_send()
        for way in (1, 2, 3):
            direct(part, way).wait_send()
        for way in range(4):
            across_cores(part, way).wait()
        return 0

    lax.fori_loop(0, PARTS, drain, 0)


def paired_call(matching, spots, w, g, m):
    _, mats, rows, cols = w.shape
    total = mats * rows
    height = total // PARTS
    dma = pltpu.SemaphoreType.DMA
    vmem = pltpu.VMEM
    return pl.pallas_call(
        functools.partial(pair_kernel, matching, mats),
        out_shape=(
            jax.ShapeDtypeStruct((total, cols), jnp.float32),
            jax.ShapeDtypeStruct((total * spots, cols), jnp.bfloat16),
        ),
        in_specs=[pl.BlockSpec(memory_space=pl.ANY)] * 3,
        out_specs=(pl.BlockSpec(memory_space=vmem), pl.BlockSpec(memory_space=vmem)),
        scratch_shapes=[
            vmem((total, cols), jnp.float32),
            vmem((total, cols), jnp.float32),
            vmem((total, cols), jnp.float32),
            vmem((PARTS, 2, SUB, LANES), jnp.float32),
            vmem((PARTS, 2, SUB, LANES), jnp.float32),
            vmem((PARTS, 2, height, cols), jnp.int16),
            vmem((PARTS, 2, height, cols), jnp.int16),
            dma((5,)), dma((PARTS,)), dma((PARTS,)), dma((PARTS,)), dma((PARTS,)),
            dma((3, PARTS)), dma((3, PARTS)), dma((4, PARTS)), dma((4, PARTS)),
        ],
        compiler_params=pltpu.CompilerParams(
            collective_id=matching, has_side_effects=True, vmem_limit_bytes=40 * 1024 * 1024
        ),
        cost_estimate=pl.CostEstimate(flops=12 * w.size, bytes_accessed=20 * w.size, transcendentals=0),
        name="matching_%d" % matching,
    )(*(a.reshape(total, cols) for a in (w, g, m)))


def publish_kernel(next_ref, full_ref, next_hbm, full_hbm, sem):
    step = full_ref.shape[0] // SLICES
    copies = [
        pltpu.make_async_copy(
            full_ref.at[pl.ds(part * step, step)], full_hbm.at[pl.ds(part * step, step)], sem.at[part]
        )
        for part in range(SLICES)
    ]
    copies.append(pltpu.make_async_copy(next_ref, next_hbm, sem.at[SLICES]))
    for copy in copies:
        copy.start()
    for copy in copies:
        copy.wait()


def publish(moment_next, full):
    return pl.pallas_call(
        publish_kernel,
        out_shape=[jax.ShapeDtypeStruct(a.shape, a.dtype) for a in (moment_next, full)],
        in_specs=[pl.BlockSpec(memory_space=pltpu.VMEM)] * 2,
        out_specs=[pl.BlockSpec(memory_space=pl.ANY)] * 2,
        scratch_shapes=[pltpu.SemaphoreType.DMA((SLICES + 1,))],
        name="publish",
    )(moment_next, full)


def paired_body(spots, outer_weights, pseudo_grad, momentum, partner):
    calls = [functools.partial(paired_call, matching, spots) for matching in (1, 2, 3)]
    moment_next, full = publish(*lax.switch(partner[0] - 1, calls, outer_weights, pseudo_grad, momentum))
    _, mats, rows, cols = momentum.shape
    return moment_next.reshape(momentum.shape), full.reshape(1, mats, rows * spots, cols)


def solution(mesh):
    workers, spots = mesh.shape["worker"], mesh.shape["fsdp"]
    body = gathered_body
    if workers == 4 and spots == 8:
        body = functools.partial(paired_body, spots)
    placed = (
        P("worker", None, "fsdp", None),
        P("worker", None, "fsdp", None),
        P("worker", None, "fsdp", None),
        P(),
    )
    return jax.shard_map(
        body,
        mesh=mesh,
        in_specs=placed,
        out_specs=(P("worker", None, "fsdp", None), P("worker", None, None, None)),
        check_vma=False,
    )
```

profile of v0, /device:TPU:11, one launch (start us, length us, event | category | flops | bytes accessed | tf_op | source)
XLA Modules:
  0.0 67.6 jit_solution(726303924948379446)
XLA Ops:
  1.3 61.7 %conditional.1 = ((f32[512,512]{1,0:T(8,128)S(1)}, bf16[4096,512]{1,0:T(8,128)(2,1)})) conditional(s32[]{:T(128)} %bitcast.9, (f32[1,2,256,512]{3,2,1,0:T(8,128)}, f32[1,2,256,512]{3,2,1,0:T(8,128)}, f32[1,2,256,512]{3,2,1,0:T(8,128)}) %tuple.17, (f32[1,2,256,512]{3,2,1,0:T(8,128)}, f32[1,2,256,512]{3,2,1,0:T(8,128)}, ...), branch_computations={%region_0.0_spmd, %region_1.0_spmd, %region_2.0_spmd} | conditional | flops 3145728 | bytes 5242888 | solution.py:299
  1.3 61.7 %matching_3.1 = (f32[512,512]{1,0:T(8,128)S(1)}, bf16[4096,512]{1,0:T(8,128)(2,1)}) custom-call(f32[512,512]{1,0:T(8,128)} %bitcast.15, f32[512,512]{1,0:T(8,128)} %bitcast.18, f32[512,512]{1,0:T(8,128)} %bitcast.21), custom_call_target="tpu_custom_call" | custom-call | flops 3145728 | bytes 5242880 | tf_op jit(solution)/shard_map/cond/branch_2_fun/matching_3/pallas_call | solution.py:244
  63.0 4.6 %publish.1 = (f32[512,512]{1,0:T(8,128)}, bf16[4096,512]{1,0:T(8,128)(2,1)}) custom-call(f32[512,512]{1,0:T(8,128)S(1)} %get-tuple-element.33.next_ref, bf16[4096,512]{1,0:T(8,128)(2,1)} %get-tuple-element.34.full_ref), custom_call_target="tpu_custom_call" | custom-call | tf_op jit(solution)/shard_map/publish/pallas_call | solution.py:287
where the time goes:
time: 67.7 us; the launch traced here: 67.6 us
  Pallas kernels  66.2 us (98%)
  between operations  1.29 us (2%)
    pallas_call x1, Pallas kernels, paired_call(): pl.pallas_call(functools.partial(pair_kernel, matching, mats), out_shape=...  61.7 us
    pallas_call x1, Pallas kernels, publish(): pl.pallas_call(publish_kernel, out_shape=[jax.ShapeDtypeStruct(a.shape, a...  4.58 us

commit v1 on v0

--- a/solution.py
+++ b/solution.py
@@ -16,8 +16,9 @@
 LANES = 128
 SUB = 8
 STEPS = 32767.0
-PARTS = 8
-LAG = 2
+PARTS = 16
+LAG = 3
+WAIT = 2
 SLICES = 4
 
 
@@ -89,6 +90,10 @@
     neighbour = place(along_x, along_y, 1 - core)
     peers = [(mate, spot), (worker, neighbour)] + [(worker, t) for t in twins[1:]]
 
+    barrier = pltpu.get_barrier_semaphore()
+    for peer in peers:
+        pl.semaphore_signal(barrier, inc=1, device_id=peer, device_id_type=MESH)
+
     def load(source, target, first, count, number):
         return pltpu.make_async_copy(
             source.at[pl.ds(first, count)], target.at[pl.ds(first, count)], load_sem.at[number]
@@ -103,10 +108,6 @@
     ]
     for copy in loads:
         copy.start()
-
-    barrier = pltpu.get_barrier_semaphore()
-    for peer in peers:
-        pl.semaphore_signal(barrier, inc=1, device_id=peer, device_id_type=MESH)
 
     def at(part):
         return pl.ds(pl.multiple_of(part * height, height), height)
@@ -132,7 +133,8 @@
             top = jnp.full((SUB, LANES), 1e-30, jnp.float32)
             for tile in tiles:
                 top = jnp.maximum(top, jnp.max(jnp.abs(tile), axis=0))
-            scale_out[part, number] = top
+            top = jnp.max(top, axis=0, keepdims=True)
+            scale_out[part, number : number + 1, :] = top
             inverse = STEPS / top
             for piece, tile in enumerate(tiles):
                 level = (tile * inverse[None] + 32768.5).astype(jnp.int32) - 32768
@@ -182,7 +184,7 @@
     def update(part):
         for copy in to_mate(part):
             copy.wait_recv()
-        back = [scale_in[part, number] * (1.0 / STEPS) for number in range(2)]
+        back = [scale_in[part, number : number + 1, :] * (1.0 / STEPS) for number in range(2)]
         mine = pl.ds(first_row(spot, part), height)
         for piece in range(pieces):
             lanes = slice(piece * LANES, (piece + 1) * LANES)
@@ -206,33 +208,30 @@
             direct(part, way).wait_recv()
             across_cores(part, way).start()
 
-    def head(part, _):
-        update(part)
-        return 0
-
-    def both(part, _):
-        update(part)
-        pass_on(part - LAG)
-        return 0
-
-    def tail(part, _):
-        pass_on(part)
-        return 0
-
-    lax.fori_loop(0, LAG, head, 0)
-    lax.fori_loop(LAG, PARTS, both, 0)
-    lax.fori_loop(PARTS - LAG, PARTS, tail, 0)
-
-    def drain(part, _):
+    def drain(part):
         for copy in to_mate(part):
             copy.wait_send()
         for way in (1, 2, 3):
             direct(part, way).wait_send()
         for way in range(4):
             across_cores(part, way).wait()
+
+    def step(part, _):
+        @pl.when(part < PARTS)
+        def _():
+            update(part)
+
+        @pl.when(jnp.logical_and(part >= LAG, part < PARTS + LAG))
+        def _():
+            pass_on(part - LAG)
+
+        @pl.when(part >= LAG + WAIT)
+        def _():
+            drain(part - LAG - WAIT)
+
         return 0
 
-    lax.fori_loop(0, PARTS, drain, 0)
+    lax.fori_loop(0, PARTS + LAG + WAIT, step, 0)
 
 
 def paired_call(matching, spots, w, g, m):
@@ -253,8 +252,8 @@
             vmem((total, cols), jnp.float32),
             vmem((total, cols), jnp.float32),
             vmem((total, cols), jnp.float32),
-            vmem((PARTS, 2, SUB, LANES), jnp.float32),
-            vmem((PARTS, 2, SUB, LANES), jnp.float32),
+            vmem((PARTS, 2, LANES), jnp.float32),
+            vmem((PARTS, 2, LANES), jnp.float32),
             vmem((PARTS, 2, height, cols), jnp.int16),
             vmem((PARTS, 2, height, cols), jnp.int16),
             dma((5,)), dma((PARTS,)), dma((PARTS,)), dma((PARTS,)), dma((PARTS,)),

time: 67.7 us -> 67.4 us (level)
  the two profiles are of different devices: /device:TPU:11 before, /device:TPU:0 now
where the time goes in v1:
time: 67.4 us; the launch traced here: 67.2 us
  Pallas kernels  65.9 us (98%)
  between operations  1.29 us (2%)
    pallas_call x1, Pallas kernels, paired_call(): pl.pallas_call(functools.partial(pair_kernel, matching, mats), out_shape=...  61.3 us
    pallas_call x1, Pallas kernels, publish(): pl.pallas_call(publish_kernel, out_shape=[jax.ShapeDtypeStruct(a.shape, a...  4.58 us

profile of v1, /device:TPU:0, one launch (start us, length us, event | category | flops | bytes accessed | tf_op | source)
XLA Modules:
  0.0 67.2 jit_solution(16945641130929415708)
XLA Ops:
  1.3 61.3 %conditional.1 = ((f32[512,512]{1,0:T(8,128)S(1)}, bf16[4096,512]{1,0:T(8,128)(2,1)})) conditional(s32[]{:T(128)} %bitcast.9, (f32[1,2,256,512]{3,2,1,0:T(8,128)}, f32[1,2,256,512]{3,2,1,0:T(8,128)}, f32[1,2,256,512]{3,2,1,0:T(8,128)}) %tuple.17, (f32[1,2,256,512]{3,2,1,0:T(8,128)}, f32[1,2,256,512]{3,2,1,0:T(8,128)}, ...), branch_computations={%region_0.0_spmd, %region_1.0_spmd, %region_2.0_spmd} | conditional | flops 3145728 | bytes 5242888 | solution.py:298
  1.3 61.3 %matching_2.1 = (f32[512,512]{1,0:T(8,128)S(1)}, bf16[4096,512]{1,0:T(8,128)(2,1)}) custom-call(f32[512,512]{1,0:T(8,128)} %bitcast.14, f32[512,512]{1,0:T(8,128)} %bitcast.17, f32[512,512]{1,0:T(8,128)} %bitcast.20), custom_call_target="tpu_custom_call" | custom-call | flops 3145728 | bytes 5242880 | tf_op jit(solution)/shard_map/cond/branch_1_fun/matching_2/pallas_call | solution.py:243
  62.6 4.6 %publish.1 = (f32[512,512]{1,0:T(8,128)}, bf16[4096,512]{1,0:T(8,128)(2,1)}) custom-call(f32[512,512]{1,0:T(8,128)S(1)} %get-tuple-element.33.next_ref, bf16[4096,512]{1,0:T(8,128)(2,1)} %get-tuple-element.34.full_ref), custom_call_target="tpu_custom_call" | custom-call | tf_op jit(solution)/shard_map/publish/pallas_call | solution.py:286
